TPU v7x, 256 devices: a whole 4x4x8 slice. The times are simulated.
256 devices in a mesh: grp: 32 (over z, y), ulys: 8 (over x, core).
Axes of the slice: x: 4, y: 4, z: 8, core: 2. Of those that a mesh axis runs over, the one named last changes fastest.
Arguments:
- layer_states: bfloat16 [32, 512, 7168], P('grp', None, 'ulys'), may hold values from -64 to 64
- new_states: bfloat16 [3, 32, 7168], P(None, 'grp', 'ulys'), may hold values from -64 to 64
- out_proj: bfloat16 [5120, 5120], P('ulys'), may hold values from -0.3125 to 0.3125
- gain: bfloat16 [5120], replicated, may hold values from 0.5 to 1.5
- lengths: int32 [32], P('grp'), may hold values from 64 to 512, as said below
- finished: int32 [32], P('grp'), may hold values from 0 to 1, as said below
- assignment: int32 [32], replicated, may hold values from 0 to 31, as said below
Outputs:
- decoded: bfloat16 [3, 32, 5120], P(None, 'grp', 'ulys')
- scored: bfloat16 [32, 512, 5120], P('grp', 'ulys')
Inputs may be any that keep to these rules, and one draw needn't show every extreme that they name: `lengths`: one row of each draw has length 512. Some row is finished and some row is not. `assignment`: for each r below 1, the entries r, 1 + r, 2 + r, ... form a permutation of the trainer groups.
All inputs are finite; a program needn't handle non-finite values.
Results may differ from a plain program's by a relative error of at most 0.019.
Values may be sent and summed in bfloat16 or wider, within the bound.
A program may use at most 64 MiB of HBM per device.

v0:
```python
import math

import jax
import jax.numpy as jnp
from jax import lax
from jax.experimental import pallas as pl
from jax.experimental.pallas import tpu as pltpu
from jax.sharding import PartitionSpec as P

HD = 128
QPK = 5
GW = 896
FEAT = QPK * HD
CACHE = 512
D = 5120
STEPS = 3
N_GRP = 32
N_ULYS = 8
N_Z = 8
N_Y = 4
PBLK = CACHE // N_ULYS
TILE = PBLK // N_Y
QBLK = 128
N_B = CACHE // QBLK
B_TILES = QBLK // TILE
PAD = 8
WCHUNK = 1280
N_W = D // WCHUNK
EXP2_SCALE = HD ** (-0.5) * math.log2(math.e)
NEG = -1e30
MIB = 1024 * 1024
MESH = pl.DeviceIdType.MESH
CHUNKS = (2, 3)
FIRST = tuple(sum(CHUNKS[:c]) for c in range(len(CHUNKS)))
N_C = len(CHUNKS)


def attend_block(x, out, b, first, count, limit):
    rows = lax.broadcasted_iota(jnp.int32, (QBLK, 1), 0)
    cols = lax.broadcasted_iota(jnp.int32, (1, QBLK), 1)
    top = b * QBLK
    span = top + QBLK
    keys = x[0:span, FEAT:FEAT + HD]
    values = x[0:span, FEAT + HD:FEAT + 2 * HD]
    live = rows + top < limit
    for j in range(count):
        q = first + j
        query = x[top:span, q * HD:(q + 1) * HD]
        s = lax.dot_general(query, keys, (((1,), (1,)), ((), ())), preferred_element_type=jnp.float32)
        diag = jnp.where(cols <= rows, s[:, top:span], NEG)
        s = diag if b == 0 else jnp.concatenate([s[:, :top], diag], axis=1)
        m = jnp.max(s, axis=1, keepdims=True)
        p = jnp.exp2((s - m) * EXP2_SCALE)
        total = jnp.sum(p, axis=1, keepdims=True)
        o = jnp.dot(p.astype(jnp.bfloat16), values, preferred_element_type=jnp.float32)
        o = jnp.where(live, o * (1.0 / total), 0.0)
        out[top:span, j * HD:(j + 1) * HD] = o.astype(jnp.bfloat16)


def decode_heads(x, fresh, dhead, length):
    keys = x[:, FEAT:FEAT + HD]
    values = x[:, FEAT + HD:FEAT + 2 * HD]
    new_keys = fresh[:, FEAT:FEAT + HD].astype(jnp.bfloat16)
    new_values = fresh[:, FEAT + HD:FEAT + 2 * HD].astype(jnp.bfloat16)
    old_mask = lax.broadcasted_iota(jnp.int32, (1, CACHE), 1) < length
    step = lax.broadcasted_iota(jnp.int32, (PAD, PAD), 0)
    new_mask = lax.broadcasted_iota(jnp.int32, (PAD, PAD), 1) <= step
    dims = (((1,), (1,)), ((), ()))
    for q in range(QPK):
        query = fresh[:, q * HD:(q + 1) * HD].astype(jnp.bfloat16)
        old = lax.dot_general(query, keys, dims, preferred_element_type=jnp.float32)
        new = lax.dot_general(query, new_keys, dims, preferred_element_type=jnp.float32)
        old = jnp.where(old_mask, old, NEG)
        new = jnp.where(new_mask, new, NEG)
        m = jnp.maximum(jnp.max(old, axis=1, keepdims=True), jnp.max(new, axis=1, keepdims=True))
        p_old = jnp.exp2((old - m) * EXP2_SCALE)
        p_new = jnp.exp2((new - m) * EXP2_SCALE)
        total = jnp.sum(p_old, axis=1, keepdims=True) + jnp.sum(p_new, axis=1, keepdims=True)
        o = jnp.dot(p_old.astype(jnp.bfloat16), values, preferred_element_type=jnp.float32)
        o = o + jnp.dot(p_new.astype(jnp.bfloat16), new_values, preferred_element_type=jnp.float32)
        dhead[:, q * HD:(q + 1) * HD] = (o * (1.0 / total)).astype(jnp.bfloat16)


def kernel(x_hbm, new_hbm, w_hbm, gain_hbm, length_s, done_s, assign_hbm, dec, scored, *scratch):
    heads, recv, stage = scratch[:N_C], scratch[N_C:2 * N_C], scratch[2 * N_C:3 * N_C]
    (raw, x, new, w, gain, assign, source, fresh, dhead, part, dec_in,
     x_sem, w_sem, small_sem, send1, recv1, send2, recv2, send3, recv3) = scratch[3 * N_C:]
    me = lax.axis_index("grp")
    u = lax.axis_index("ulys")
    z = me // N_Y
    y = me % N_Y
    i_in = (u - z + N_Z) % N_Z
    g_in = (2 * z - u + N_Z) % N_Z
    b_in = (y - i_in + 2 * N_Y) % N_Y
    p_out = 2 * b_in + i_in // N_Y
    r_out = i_in % N_Y
    hit1 = jnp.where(g_in == u, 1, 0)
    hit2 = jnp.where(p_out == u, 1, 0)

    small = [
        pltpu.make_async_copy(src, dst, small_sem.at[k])
        for k, (src, dst) in enumerate(
            ((assign_hbm, assign), (new_hbm, new), (gain_hbm, gain)))
    ]
    x_copies = [
        pltpu.make_async_copy(x_hbm.at[0, pl.ds(b * QBLK, QBLK)], x.at[pl.ds(b * QBLK, QBLK)], x_sem.at[b])
        for b in range(N_B)
    ]
    w_copies = [
        pltpu.make_async_copy(w_hbm.at[:, pl.ds(c * WCHUNK, WCHUNK)], w.at[c], w_sem.at[c]) for c in range(N_W)
    ]
    for copy in x_copies[:1] + small + x_copies[1:] + w_copies:
        copy.start()

    barrier = pltpu.get_barrier_semaphore()

    def greet(grp, ulys):
        pl.semaphore_signal(barrier, inc=1, device_id=(grp, ulys), device_id_type=MESH)

    @pl.loop(0, N_GRP)
    def _(n):
        @pl.when(jnp.logical_not((n == me) & (g_in == u)))
        def _():
            greet(n, g_in)

        g = n // N_Y
        i = N_Y * (u % 2) + n % N_Y
        grp = ((g + i) % N_Z) * N_Y + (u // 2 + i) % N_Y
        ulys = (g + 2 * i) % N_ULYS

        @pl.when(jnp.logical_not((grp == me) & (ulys == u)))
        def _():
            greet(grp, ulys)

    @pl.loop(1, N_ULYS)
    def _(k):
        greet(me, (u + k) % N_ULYS)

    length = length_s[0]
    done = done_s[0]
    limit = length * done

    for c in range(N_C):
        for b in range(N_B):
            if c == 0:
                x_copies[b].wait()
            attend_block(x, heads[c], b, FIRST[c], CHUNKS[c], limit)
            if c == 0 and b == 0:
                pl.semaphore_wait(barrier, 2 * N_GRP - hit1 - hit2 + N_ULYS - 1)

            @pl.loop(0, B_TILES)
            def _(k, c=c, b=b):
                i = (k + y + z) % B_TILES
                grp = ((u + i) % N_Z) * N_Y + (b + i) % N_Y
                ulys = (u + 2 * i) % N_ULYS
                src = heads[c].at[pl.ds(pl.multiple_of(b * QBLK + i * TILE, TILE), TILE)]
                own = (grp == me) & (ulys == u)

                @pl.when(own)
                def _():
                    pltpu.make_async_copy(src, recv[c].at[me], recv1.at[c]).start()

                @pl.when(jnp.logical_not(own))
                def _():
                    pltpu.make_async_remote_copy(
                        src, recv[c].at[me], send1.at[c], recv1.at[c], device_id=(grp, ulys), device_id_type=MESH
                    ).start()

    small[0].wait()

    @pl.loop(0, N_GRP)
    def _(t):
        found = 0
        for n in range(N_GRP):
            found = jnp.where(assign[n] == t, n, found)
        source[t] = found

    small[1].wait()
    fresh[...] = jnp.zeros_like(fresh)
    fresh[0:STEPS, :] = new[...].astype(jnp.float32)
    decode_heads(x, fresh, dhead, length)
    lhs = dhead[...]
    for c in range(N_W):
        w_copies[c].wait()
        part[:, c * WCHUNK:(c + 1) * WCHUNK] = jnp.dot(lhs, w[c], preferred_element_type=jnp.float32)

    @pl.loop(1, N_ULYS)
    def _(k):
        p = (u + k) % N_ULYS
        pltpu.make_async_remote_copy(
            part.at[:, pl.ds(pl.multiple_of(p * FEAT, HD), FEAT)],
            dec_in.at[u], send3, recv3, device_id=(me, p), device_id_type=MESH
        ).start()

    pltpu.make_async_copy(part.at[:, pl.ds(pl.multiple_of(u * FEAT, HD), FEAT)], dec_in.at[u], recv3).start()

    rows = pl.ds(pl.multiple_of(r_out * TILE, TILE), TILE)
    for c in range(N_C):
        width = CHUNKS[c] * HD
        cols = pl.ds(pl.multiple_of(g_in * FEAT + FIRST[c] * HD, HD), width)
        pltpu.make_async_copy(recv[c], recv[c], recv1.at[c]).wait()

        @pl.loop(0, N_GRP)
        def _(k, c=c, cols=cols):
            t = (me + k) % N_GRP
            stage[c][t] = recv[c][source[t]]
            own = (t == me) & (p_out == u)

            @pl.when(own)
            def _():
                pltpu.make_async_copy(stage[c].at[t], raw.at[rows, cols], recv2.at[c]).start()

            @pl.when(jnp.logical_not(own))
            def _():
                pltpu.make_async_remote_copy(
                    stage[c].at[t], raw.at[rows, cols], send2.at[c], recv2.at[c],
                    device_id=(t, p_out), device_id_type=MESH
                ).start()

    pltpu.make_async_copy(dec_in, dec_in, recv3).wait()
    total = dec_in[0]
    for g in range(1, N_ULYS):
        total = total + dec_in[g]
    dec[...] = (total * (1 - done).astype(jnp.float32))[0:STEPS].astype(jnp.bfloat16)

    small[2].wait()
    square = jnp.zeros((PBLK, HD), jnp.float32)
    for c in range(N_C):
        pltpu.make_async_copy(recv[c], recv[c], recv2.at[c]).wait()
        for g in range(N_ULYS):
            for q in range(FIRST[c], FIRST[c] + CHUNKS[c]):
                at = (g * QPK + q) * HD
                part_of = raw[:, at:at + HD].astype(jnp.float32)
                square = square + part_of * part_of
    power = jnp.sum(square, axis=1, keepdims=True) * (1.0 / D)
    factor = lax.rsqrt(power + 1e-06)
    gains = gain[...].astype(jnp.float32)
    for k in range(D // HD):
        lifted = raw[:, k * HD:(k + 1) * HD].astype(jnp.float32)
        scored[:, k * HD:(k + 1) * HD] = (lifted * factor * gains[k:k + 1]).astype(jnp.bfloat16)

    for sems, hit in ((send1, hit1), (send2, hit2)):
        for c in range(N_C):
            @pl.when(hit > 0)
            def _(c=c, sems=sems):
                sent = stage[c].at[pl.ds(0, N_GRP - 1)]
                pltpu.make_async_copy(sent, sent, sems.at[c]).wait()

            @pl.when(hit <= 0)
            def _(c=c, sems=sems):
                pltpu.make_async_copy(stage[c], stage[c], sems.at[c]).wait()
    sent = dec_in.at[pl.ds(0, N_ULYS - 1)]
    pltpu.make_async_copy(sent, sent, send3).wait()


def body(layer_states, new_states, out_proj, gain, lengths, finished, assignment):
    hbm = pl.BlockSpec(memory_space=pltpu.HBM)
    smem = pl.BlockSpec(memory_space=pltpu.SMEM)
    vmem = pl.BlockSpec(memory_space=pltpu.VMEM)
    dec, scored = pl.pallas_call(
        kernel,
        out_shape=(
            jax.ShapeDtypeStruct((STEPS, FEAT), jnp.bfloat16),
            jax.ShapeDtypeStruct((PBLK, D), jnp.bfloat16),
        ),
        in_specs=[hbm] * 4 + [smem] * 2 + [hbm],
        out_specs=(vmem, vmem),
        scratch_shapes=[pltpu.VMEM((CACHE, n * HD), jnp.bfloat16) for n in CHUNKS]
        + [pltpu.VMEM((N_GRP, TILE, n * HD), jnp.bfloat16) for n in CHUNKS] * 2
        + [
            pltpu.VMEM((PBLK, D), jnp.bfloat16),
            pltpu.VMEM((CACHE, GW), jnp.bfloat16),
            pltpu.VMEM((STEPS, GW), jnp.bfloat16),
            pltpu.VMEM((N_W, FEAT, WCHUNK), jnp.bfloat16),
            pltpu.VMEM((D // HD, HD), jnp.bfloat16),
            pltpu.SMEM((N_GRP,), jnp.int32),
            pltpu.SMEM((N_GRP,), jnp.int32),
            pltpu.VMEM((PAD, GW), jnp.float32),
            pltpu.VMEM((PAD, FEAT), jnp.bfloat16),
            pltpu.VMEM((PAD, D), jnp.float32),
            pltpu.VMEM((N_ULYS, PAD, FEAT), jnp.float32),
            pltpu.SemaphoreType.DMA((N_B,)),
            pltpu.SemaphoreType.DMA((N_W,)),
            pltpu.SemaphoreType.DMA((3,)),
        ]
        + [pltpu.SemaphoreType.DMA((N_C,))] * 4
        + [pltpu.SemaphoreType.DMA] * 2,
        compiler_params=pltpu.CompilerParams(
            vmem_limit_bytes=56 * MIB, collective_id=0, has_side_effects=True
        ),
        name="step",
    )(layer_states, new_states.reshape(STEPS, GW), out_proj, gain.reshape(D // HD, HD), lengths, finished, assignment)
    return (dec.reshape(STEPS, 1, FEAT), scored.reshape(1, PBLK, D))


def solution(mesh):
    placed = (
        P("grp", None, "ulys"),
        P(None, "grp", "ulys"),
        P("ulys", None),
        P(),
        P("grp"),
        P("grp"),
        P(),
    )
    return jax.shard_map(
        body,
        mesh=mesh,
        in_specs=placed,
        out_specs=(P(None, "grp", "ulys"), P("grp", "ulys", None)),
        check_vma=False,
    )
```

profile of v0, /device:TPU:8, one launch (start us, length us, event | category | flops | bytes accessed | tf_op | source)
XLA Modules:
  0.0 49.8 jit_solution(15497099372832728251)
XLA Ops:
  1.9 44.6 %step.1 = (bf16[3,640]{1,0:T(4,128)(2,1)}, bf16[64,5120]{1,0:T(8,128)(2,1)}) custom-call(bf16[1,512,896]{2,1,0:T(8,128)(2,1)} %x_hbm.1, bf16[3,896]{1,0:T(4,128)(2,1)} %bitcast.6, bf16[640,5120]{1,0:T(8,128)(2,1)} %w_hbm.1, bf16[40,128]{1,0:T(8,128)(2,1)} %bitcast.5, s32[1]{0:T(128)S(6)} %copy.11.length_s, s32[1]{0:T(128)S(6)} %copy.12.done_s, s32[32]{0:T(128)} %assign_hbm.1), custom_call_target="tpu_custom_call" | custom-call | tf_op jit(solution)/shard_map/step/pallas_call | solution.py:260
  46.5 1.3 %copy.13 = bf16[3,1,640]{2,0,1:T(4,128)(2,1)} copy(bf16[3,1,640]{2,0,1:T(4,128)(2,1)} %bitcast.7) | data formatting | bytes 7680
  47.8 2.0 %copy.14 = bf16[1,64,5120]{2,1,0:T(8,128)(2,1)} copy(bf16[1,64,5120]{2,1,0:T(8,128)(2,1)} %bitcast.4) | data formatting | bytes 1310720
where the time goes:
time: 50 us; the launch traced here: 49.8 us
  Pallas kernels  44.6 us (89%)
  local copies, waits for them, and re-layouts  3.25 us (6%)
  between operations  1.93 us (4%)
    pallas_call x1, Pallas kernels, body(): pl.pallas_call(kernel, out_shape=(jax.ShapeDtypeStruct((STEPS, FEAT), jnp...  44.6 us
    unnamed x2, local copies, waits for them, and re-layouts  3.25 us

commit v1 on v0

--- a/solution.py
+++ b/solution.py
@@ -31,8 +31,21 @@
 MIB = 1024 * 1024
 MESH = pl.DeviceIdType.MESH
 CHUNKS = (2, 3)
+OUT = pltpu.VMEM
+VLIM = 32
 FIRST = tuple(sum(CHUNKS[:c]) for c in range(len(CHUNKS)))
 N_C = len(CHUNKS)
+
+
+def relay_of(head, b, i):
+    p = 2 * b + i // N_Y
+    return ((head + p) % N_Z) * N_Y + (b + i) % N_Y, p
+
+
+def tile_of(z, y, u):
+    b = u // 2
+    r = (y - b + N_Y) % N_Y
+    return (z - u + N_Z) % N_Z, b, (u % 2) * N_Y + r
 
 
 def attend_block(x, out, b, first, count, limit):
@@ -81,17 +94,15 @@
         dhead[:, q * HD:(q + 1) * HD] = (o * (1.0 / total)).astype(jnp.bfloat16)
 
 
-def kernel(x_hbm, new_hbm, w_hbm, gain_hbm, length_s, done_s, assign_hbm, dec, scored, *scratch):
+def step_kernel(x_hbm, new_hbm, w_hbm, length_s, done_s, assign_hbm, dec, raw, *scratch):
     heads, recv, stage = scratch[:N_C], scratch[N_C:2 * N_C], scratch[2 * N_C:3 * N_C]
-    (raw, x, new, w, gain, assign, source, fresh, dhead, part, dec_in,
+    (x, new, w, assign, found, source, fresh, dhead, part, dec_in,
      x_sem, w_sem, small_sem, send1, recv1, send2, recv2, send3, recv3) = scratch[3 * N_C:]
     me = lax.axis_index("grp")
     u = lax.axis_index("ulys")
     z = me // N_Y
     y = me % N_Y
-    i_in = (u - z + N_Z) % N_Z
-    g_in = (2 * z - u + N_Z) % N_Z
-    b_in = (y - i_in + 2 * N_Y) % N_Y
+    g_in, b_in, i_in = tile_of(z, y, u)
     p_out = 2 * b_in + i_in // N_Y
     r_out = i_in % N_Y
     hit1 = jnp.where(g_in == u, 1, 0)
@@ -100,7 +111,7 @@
     small = [
         pltpu.make_async_copy(src, dst, small_sem.at[k])
         for k, (src, dst) in enumerate(
-            ((assign_hbm, assign), (new_hbm, new), (gain_hbm, gain)))
+            ((assign_hbm, assign), (new_hbm, new)))
     ]
     x_copies = [
         pltpu.make_async_copy(x_hbm.at[0, pl.ds(b * QBLK, QBLK)], x.at[pl.ds(b * QBLK, QBLK)], x_sem.at[b])
@@ -117,16 +128,13 @@
     def greet(grp, ulys):
         pl.semaphore_signal(barrier, inc=1, device_id=(grp, ulys), device_id_type=MESH)
 
-    @pl.loop(0, N_GRP)
+    @pl.loop(0, N_GRP, unroll=8)
     def _(n):
         @pl.when(jnp.logical_not((n == me) & (g_in == u)))
         def _():
             greet(n, g_in)
 
-        g = n // N_Y
-        i = N_Y * (u % 2) + n % N_Y
-        grp = ((g + i) % N_Z) * N_Y + (u // 2 + i) % N_Y
-        ulys = (g + 2 * i) % N_ULYS
+        grp, ulys = relay_of(n // N_Y, u // 2, N_Y * (u % 2) + n % N_Y)
 
         @pl.when(jnp.logical_not((grp == me) & (ulys == u)))
         def _():
@@ -145,54 +153,37 @@
             if c == 0:
                 x_copies[b].wait()
             attend_block(x, heads[c], b, FIRST[c], CHUNKS[c], limit)
-            if c == 0 and b == 0:
-                pl.semaphore_wait(barrier, 2 * N_GRP - hit1 - hit2 + N_ULYS - 1)
-
-            @pl.loop(0, B_TILES)
-            def _(k, c=c, b=b):
-                i = (k + y + z) % B_TILES
-                grp = ((u + i) % N_Z) * N_Y + (b + i) % N_Y
-                ulys = (u + 2 * i) % N_ULYS
-                src = heads[c].at[pl.ds(pl.multiple_of(b * QBLK + i * TILE, TILE), TILE)]
-                own = (grp == me) & (ulys == u)
-
-                @pl.when(own)
-                def _():
-                    pltpu.make_async_copy(src, recv[c].at[me], recv1.at[c]).start()
-
-                @pl.when(jnp.logical_not(own))
-                def _():
-                    pltpu.make_async_remote_copy(
-                        src, recv[c].at[me], send1.at[c], recv1.at[c], device_id=(grp, ulys), device_id_type=MESH
-                    ).start()
+        if c == 0:
+            pl.semaphore_wait(barrier, 2 * N_GRP - hit1 - hit2 + N_ULYS - 1)
+
+        @pl.loop(0, N_GRP)
+        def _(k, c=c):
+            b = (k // B_TILES + z + y) % N_B
+            i = (k + y + z) % B_TILES
+            grp, ulys = relay_of(u, b, i)
+            src = heads[c].at[pl.ds(pl.multiple_of(b * QBLK + i * TILE, TILE), TILE)]
+            own = (grp == me) & (ulys == u)
+
+            @pl.when(own)
+            def _():
+                pltpu.make_async_copy(src, recv[c].at[me], recv1.at[c]).start()
+
+            @pl.when(jnp.logical_not(own))
+            def _():
+                pltpu.make_async_remote_copy(
+                    src, recv[c].at[me], send1.at[c], recv1.at[c], device_id=(grp, ulys), device_id_type=MESH
+                ).start()
 
     small[0].wait()
-
-    @pl.loop(0, N_GRP)
-    def _(t):
-        found = 0
-        for n in range(N_GRP):
-            found = jnp.where(assign[n] == t, n, found)
-        source[t] = found
-
-    small[1].wait()
-    fresh[...] = jnp.zeros_like(fresh)
-    fresh[0:STEPS, :] = new[...].astype(jnp.float32)
-    decode_heads(x, fresh, dhead, length)
-    lhs = dhead[...]
-    for c in range(N_W):
-        w_copies[c].wait()
-        part[:, c * WCHUNK:(c + 1) * WCHUNK] = jnp.dot(lhs, w[c], preferred_element_type=jnp.float32)
-
-    @pl.loop(1, N_ULYS)
-    def _(k):
-        p = (u + k) % N_ULYS
-        pltpu.make_async_remote_copy(
-            part.at[:, pl.ds(pl.multiple_of(p * FEAT, HD), FEAT)],
-            dec_in.at[u], send3, recv3, device_id=(me, p), device_id_type=MESH
-        ).start()
-
-    pltpu.make_async_copy(part.at[:, pl.ds(pl.multiple_of(u * FEAT, HD), FEAT)], dec_in.at[u], recv3).start()
+    place = lax.broadcasted_iota(jnp.int32, (N_GRP, HD), 0)
+    group = jnp.zeros((N_GRP, HD), jnp.int32)
+    for n in range(N_GRP):
+        group = jnp.where(place == n, assign[n], group)
+    lanes = lax.broadcasted_iota(jnp.int32, (N_GRP, HD), 1)
+    found[...] = jnp.max(jnp.where(group == lanes, place, 0), axis=0, keepdims=True)
+    to_scalars = pltpu.make_async_copy(found, source, small_sem.at[0])
+    to_scalars.start()
+    to_scalars.wait()
 
     rows = pl.ds(pl.multiple_of(r_out * TILE, TILE), TILE)
     for c in range(N_C):
@@ -202,8 +193,8 @@
 
         @pl.loop(0, N_GRP)
         def _(k, c=c, cols=cols):
-            t = (me + k) % N_GRP
-            stage[c][t] = recv[c][source[t]]
+            t = (k // 4) * N_Y + (k + y) % N_Y
+            stage[c][t] = recv[c][source[0, t]]
             own = (t == me) & (p_out == u)
 
             @pl.when(own)
@@ -217,28 +208,35 @@
                     device_id=(t, p_out), device_id_type=MESH
                 ).start()
 
+        if c > 0:
+            continue
+        small[1].wait()
+        fresh[...] = jnp.zeros_like(fresh)
+        fresh[0:STEPS, :] = new[...].astype(jnp.float32)
+        decode_heads(x, fresh, dhead, length)
+        lhs = dhead[...]
+        for k in range(N_W):
+            w_copies[k].wait()
+            part[:, k * WCHUNK:(k + 1) * WCHUNK] = jnp.dot(lhs, w[k], preferred_element_type=jnp.float32)
+
+        @pl.loop(1, N_ULYS)
+        def _(k):
+            p = (u + k) % N_ULYS
+            pltpu.make_async_remote_copy(
+                part.at[:, pl.ds(pl.multiple_of(p * FEAT, HD), FEAT)],
+                dec_in.at[u], send3, recv3, device_id=(me, p), device_id_type=MESH
+            ).start()
+
+        pltpu.make_async_copy(part.at[:, pl.ds(pl.multiple_of(u * FEAT, HD), FEAT)], dec_in.at[u], recv3).start()
+
     pltpu.make_async_copy(dec_in, dec_in, recv3).wait()
     total = dec_in[0]
     for g in range(1, N_ULYS):
         total = total + dec_in[g]
     dec[...] = (total * (1 - done).astype(jnp.float32))[0:STEPS].astype(jnp.bfloat16)
 
-    small[2].wait()
-    square = jnp.zeros((PBLK, HD), jnp.float32)
     for c in range(N_C):
         pltpu.make_async_copy(recv[c], recv[c], recv2.at[c]).wait()
-        for g in range(N_ULYS):
-            for q in range(FIRST[c], FIRST[c] + CHUNKS[c]):
-                at = (g * QPK + q) * HD
-                part_of = raw[:, at:at + HD].astype(jnp.float32)
-                square = square + part_of * part_of
-    power = jnp.sum(square, axis=1, keepdims=True) * (1.0 / D)
-    factor = lax.rsqrt(power + 1e-06)
-    gains = gain[...].astype(jnp.float32)
-    for k in range(D // HD):
-        lifted = raw[:, k * HD:(k + 1) * HD].astype(jnp.float32)
-        scored[:, k * HD:(k + 1) * HD] = (lifted * factor * gains[k:k + 1]).astype(jnp.bfloat16)
-
     for sems, hit in ((send1, hit1), (send2, hit2)):
         for c in range(N_C):
             @pl.when(hit > 0)
@@ -253,44 +251,84 @@
     pltpu.make_async_copy(sent, sent, send3).wait()
 
 
+def norm_kernel(raw, dec, gain, decoded, scored, out, sem):
+    decoded[...] = dec[...]
+    gains = gain[...].astype(jnp.float32)
+    copies = []
+    for r in range(N_Y):
+        rows = slice(r * TILE, (r + 1) * TILE)
+        square = jnp.zeros((TILE, HD), jnp.float32)
+        for k in range(D // HD):
+            lifted = raw[rows, k * HD:(k + 1) * HD].astype(jnp.float32)
+            square = square + lifted * lifted
+        power = jnp.sum(square, axis=1, keepdims=True) * (1.0 / D)
+        factor = lax.rsqrt(power + 1e-06)
+        for k in range(D // HD):
+            lifted = raw[rows, k * HD:(k + 1) * HD].astype(jnp.float32)
+            out[rows, k * HD:(k + 1) * HD] = (lifted * factor * gains[k:k + 1]).astype(jnp.bfloat16)
+        at = pl.ds(r * TILE, TILE)
+        copies.append(pltpu.make_async_copy(out.at[at], scored.at[at], sem.at[r]))
+        copies[-1].start()
+    for copy in copies:
+        copy.wait()
+
+
 def body(layer_states, new_states, out_proj, gain, lengths, finished, assignment):
-    hbm = pl.BlockSpec(memory_space=pltpu.HBM)
+    hbm = pl.BlockSpec(memory_space=pl.ANY)
+    vmem = pl.BlockSpec(memory_space=pltpu.VMEM)
     smem = pl.BlockSpec(memory_space=pltpu.SMEM)
-    vmem = pl.BlockSpec(memory_space=pltpu.VMEM)
-    dec, scored = pl.pallas_call(
-        kernel,
+
+    def pinned(a):
+        return pltpu.with_memory_space_constraint(a, pltpu.HBM)
+
+    dec, raw = pl.pallas_call(
+        step_kernel,
         out_shape=(
-            jax.ShapeDtypeStruct((STEPS, FEAT), jnp.bfloat16),
-            jax.ShapeDtypeStruct((PBLK, D), jnp.bfloat16),
+            OUT((STEPS, FEAT), jnp.bfloat16),
+            OUT((PBLK, D), jnp.bfloat16),
         ),
-        in_specs=[hbm] * 4 + [smem] * 2 + [hbm],
+        in_specs=[hbm] * 3 + [smem] * 2 + [hbm],
         out_specs=(vmem, vmem),
         scratch_shapes=[pltpu.VMEM((CACHE, n * HD), jnp.bfloat16) for n in CHUNKS]
         + [pltpu.VMEM((N_GRP, TILE, n * HD), jnp.bfloat16) for n in CHUNKS] * 2
         + [
-            pltpu.VMEM((PBLK, D), jnp.bfloat16),
             pltpu.VMEM((CACHE, GW), jnp.bfloat16),
             pltpu.VMEM((STEPS, GW), jnp.bfloat16),
             pltpu.VMEM((N_W, FEAT, WCHUNK), jnp.bfloat16),
-            pltpu.VMEM((D // HD, HD), jnp.bfloat16),
             pltpu.SMEM((N_GRP,), jnp.int32),
-            pltpu.SMEM((N_GRP,), jnp.int32),
+            pltpu.VMEM((1, HD), jnp.int32),
+            pltpu.SMEM((1, HD), jnp.int32),
             pltpu.VMEM((PAD, GW), jnp.float32),
             pltpu.VMEM((PAD, FEAT), jnp.bfloat16),
             pltpu.VMEM((PAD, D), jnp.float32),
             pltpu.VMEM((N_ULYS, PAD, FEAT), jnp.float32),
             pltpu.SemaphoreType.DMA((N_B,)),
             pltpu.SemaphoreType.DMA((N_W,)),
-            pltpu.SemaphoreType.DMA((3,)),
+            pltpu.SemaphoreType.DMA((2,)),
         ]
         + [pltpu.SemaphoreType.DMA((N_C,))] * 4
         + [pltpu.SemaphoreType.DMA] * 2,
         compiler_params=pltpu.CompilerParams(
-            vmem_limit_bytes=56 * MIB, collective_id=0, has_side_effects=True
+            vmem_limit_bytes=VLIM * MIB, collective_id=0, has_side_effects=True
         ),
         name="step",
-    )(layer_states, new_states.reshape(STEPS, GW), out_proj, gain.reshape(D // HD, HD), lengths, finished, assignment)
-    return (dec.reshape(STEPS, 1, FEAT), scored.reshape(1, PBLK, D))
+    )(
+        pinned(layer_states), pinned(new_states.reshape(STEPS, GW)), pinned(out_proj),
+        lengths, finished, pinned(assignment),
+    )
+    decoded, scored = pl.pallas_call(
+        norm_kernel,
+        out_shape=(
+            jax.ShapeDtypeStruct((STEPS, FEAT), jnp.bfloat16),
+            jax.ShapeDtypeStruct((PBLK, D), jnp.bfloat16),
+        ),
+        in_specs=[vmem] * 3,
+        out_specs=(vmem, hbm),
+        scratch_shapes=[pltpu.VMEM((PBLK, D), jnp.bfloat16), pltpu.SemaphoreType.DMA((N_Y,))],
+        compiler_params=pltpu.CompilerParams(vmem_limit_bytes=8 * MIB),
+        name="norm",
+    )(raw, dec, gain.reshape(D // HD, HD))
+    return (decoded.reshape(STEPS, 1, FEAT), scored.reshape(1, PBLK, D))
 
 
 def solution(mesh):

time: 50 us -> 46 us (0.920)
  the two profiles are of different devices: /device:TPU:8 before, /device:TPU:65 now
where the time goes in v1:
time: 46 us; the launch traced here: 45.5 us
  Pallas kernels  43.6 us (95%)
  between operations  1.96 us (4%)
    pallas_call x1, Pallas kernels, body(): pl.pallas_call(step_kernel, out_shape=(OUT((STEPS, FEAT), jnp.bfloat16),...  41.9 us
    pallas_call x1, Pallas kernels, body(): pl.pallas_call(norm_kernel, out_shape=(jax.ShapeDtypeStruct((STEPS, FEAT)...  1.66 us

profile of v1, /device:TPU:65, one launch (start us, length us, event | category | flops | bytes accessed | tf_op | source)
XLA Modules:
  0.0 45.5 jit_solution(11339647736591671257)
XLA Ops:
  0.6 0.0 copy-start
  1.9 41.9 %step.1 = (bf16[3,640]{1,0:T(4,128)(2,1)S(1)}, bf16[64,5120]{1,0:T(8,128)(2,1)S(1)}) custom-call(bf16[1,512,896]{2,1,0:T(8,128)(2,1)} %x_hbm.1, bf16[3,896]{1,0:T(4,128)(2,1)} %bitcast.5, bf16[640,5120]{1,0:T(8,128)(2,1)} %w_hbm.1, s32[1]{0:T(128)S(6)} %copy.9.length_s, s32[1]{0:T(128)S(6)} %copy.10.done_s, s32[32]{0:T(128)} %assign_hbm.1), custom_call_target="tpu_custom_call" | custom-call | tf_op jit(solution)/shard_map/step/pallas_call | solution.py:284
  43.9 0.0 copy-done
  43.9 1.7 %norm.1 = (bf16[3,640]{1,0:T(4,128)(2,1)}, bf16[64,5120]{1,0:T(8,128)(2,1)}) custom-call(bf16[64,5120]{1,0:T(8,128)(2,1)S(1)} %get-tuple-element.6.raw, bf16[3,640]{1,0:T(4,128)(2,1)S(1)} %get-tuple-element.7.dec, bf16[40,128]{1,0:T(8,128)(2,1)S(1)} %bitcast.4), custom_call_target="tpu_custom_call" | custom-call | tf_op jit(solution)/shard_map/norm/pallas_call | solution.py:319
Async XLA Ops:
  0.6 43.2 %copy-start = (bf16[5120]{0:T(1024)(128)(2,1)S(1)}, bf16[5120]{0:T(1024)(128)(2,1)}, u32[]{:S(2)}) copy-start(bf16[5120]{0:T(1024)(128)(2,1)} %param.10) | copy-start | bytes 30724

commit v2 on v1

--- a/solution.py
+++ b/solution.py
@@ -31,7 +31,7 @@
 MIB = 1024 * 1024
 MESH = pl.DeviceIdType.MESH
 CHUNKS = (2, 3)
-OUT = pltpu.VMEM
+
 VLIM = 32
 FIRST = tuple(sum(CHUNKS[:c]) for c in range(len(CHUNKS)))
 N_C = len(CHUNKS)
@@ -134,12 +134,6 @@
         def _():
             greet(n, g_in)
 
-        grp, ulys = relay_of(n // N_Y, u // 2, N_Y * (u % 2) + n % N_Y)
-
-        @pl.when(jnp.logical_not((grp == me) & (ulys == u)))
-        def _():
-            greet(grp, ulys)
-
     @pl.loop(1, N_ULYS)
     def _(k):
         greet(me, (u + k) % N_ULYS)
@@ -154,7 +148,7 @@
                 x_copies[b].wait()
             attend_block(x, heads[c], b, FIRST[c], CHUNKS[c], limit)
         if c == 0:
-            pl.semaphore_wait(barrier, 2 * N_GRP - hit1 - hit2 + N_ULYS - 1)
+            pl.semaphore_wait(barrier, N_GRP - hit1 + N_ULYS - 1)
 
         @pl.loop(0, N_GRP)
         def _(k, c=c):
@@ -193,7 +187,7 @@
 
         @pl.loop(0, N_GRP)
         def _(k, c=c, cols=cols):
-            t = (k // 4) * N_Y + (k + y) % N_Y
+            t = k
             stage[c][t] = recv[c][source[0, t]]
             own = (t == me) & (p_out == u)
 
@@ -252,9 +246,9 @@
 
 
 def norm_kernel(raw, dec, gain, decoded, scored, out, sem):
-    decoded[...] = dec[...]
+    copies = [pltpu.make_async_copy(dec, decoded, sem.at[N_Y])]
+    copies[0].start()
     gains = gain[...].astype(jnp.float32)
-    copies = []
     for r in range(N_Y):
         rows = slice(r * TILE, (r + 1) * TILE)
         square = jnp.zeros((TILE, HD), jnp.float32)
@@ -284,8 +278,8 @@
     dec, raw = pl.pallas_call(
         step_kernel,
         out_shape=(
-            OUT((STEPS, FEAT), jnp.bfloat16),
-            OUT((PBLK, D), jnp.bfloat16),
+            pltpu.VMEM((STEPS, FEAT), jnp.bfloat16),
+            pltpu.VMEM((PBLK, D), jnp.bfloat16),
         ),
         in_specs=[hbm] * 3 + [smem] * 2 + [hbm],
         out_specs=(vmem, vmem),
@@ -323,8 +317,8 @@
             jax.ShapeDtypeStruct((PBLK, D), jnp.bfloat16),
         ),
         in_specs=[vmem] * 3,
-        out_specs=(vmem, hbm),
-        scratch_shapes=[pltpu.VMEM((PBLK, D), jnp.bfloat16), pltpu.SemaphoreType.DMA((N_Y,))],
+        out_specs=(hbm, hbm),
+        scratch_shapes=[pltpu.VMEM((PBLK, D), jnp.bfloat16), pltpu.SemaphoreType.DMA((N_Y + 1,))],
         compiler_params=pltpu.CompilerParams(vmem_limit_bytes=8 * MIB),
         name="norm",
     )(raw, dec, gain.reshape(D // HD, HD))

time: 46 us -> 44.3 us (0.963)
  Pallas kernels: 43.6 us -> 41.7 us
    pallas_call x1, Pallas kernels: 41.9 us -> 40.6 us  [body(): pl.pallas_call(step_kernel, out_shape=(pltpu.VMEM((STEPS, FEAT), jnp.bflo...]
    pallas_call x1, Pallas kernels: 1.66 us -> 1.08 us  [body(): pl.pallas_call(norm_kernel, out_shape=(jax.ShapeDtypeStruct((STEPS, FEAT)...]
where the time goes in v2:
time: 44.3 us; the launch traced here: 43.7 us
  Pallas kernels  41.7 us (94%)
  between operations  1.96 us (4%)
    pallas_call x1, Pallas kernels, body(): pl.pallas_call(step_kernel, out_shape=(pltpu.VMEM((STEPS, FEAT), jnp.bflo...  40.6 us
    pallas_call x1, Pallas kernels, body(): pl.pallas_call(norm_kernel, out_shape=(jax.ShapeDtypeStruct((STEPS, FEAT)...  1.08 us

profile of v2, /device:TPU:65, one launch (start us, length us, event | category | flops | bytes accessed | tf_op | source)
XLA Modules:
  0.0 43.7 jit_solution(5974968187082815711)
XLA Ops:
  0.6 0.0 copy-start
  1.9 40.6 %step.1 = (bf16[3,640]{1,0:T(4,128)(2,1)S(1)}, bf16[64,5120]{1,0:T(8,128)(2,1)S(1)}) custom-call(bf16[1,512,896]{2,1,0:T(8,128)(2,1)} %x_hbm.1, bf16[3,896]{1,0:T(4,128)(2,1)} %bitcast.5, bf16[640,5120]{1,0:T(8,128)(2,1)} %w_hbm.1, s32[1]{0:T(128)S(6)} %copy.9.length_s, s32[1]{0:T(128)S(6)} %copy.10.done_s, s32[32]{0:T(128)} %assign_hbm.1), custom_call_target="tpu_custom_call" | custom-call | tf_op jit(solution)/shard_map/step/pallas_call | solution.py:278
  42.6 0.0 copy-done
  42.6 1.1 %norm.1 = (bf16[3,640]{1,0:T(4,128)(2,1)}, bf16[64,5120]{1,0:T(8,128)(2,1)}) custom-call(bf16[64,5120]{1,0:T(8,128)(2,1)S(1)} %get-tuple-element.6.raw, bf16[3,640]{1,0:T(4,128)(2,1)S(1)} %get-tuple-element.7.dec, bf16[40,128]{1,0:T(8,128)(2,1)S(1)} %bitcast.4), custom_call_target="tpu_custom_call" | custom-call | tf_op jit(solution)/shard_map/norm/pallas_call | solution.py:313
Async XLA Ops:
  0.6 42.0 %copy-start = (bf16[5120]{0:T(1024)(128)(2,1)S(1)}, bf16[5120]{0:T(1024)(128)(2,1)}, u32[]{:S(2)}) copy-start(bf16[5120]{0:T(1024)(128)(2,1)} %param.10) | copy-start | bytes 30724

commit v3 on v2

--- a/solution.py
+++ b/solution.py
@@ -32,14 +32,22 @@
 MESH = pl.DeviceIdType.MESH
 CHUNKS = (2, 3)
 
-VLIM = 32
+
 FIRST = tuple(sum(CHUNKS[:c]) for c in range(len(CHUNKS)))
 N_C = len(CHUNKS)
 
 
+def div(a, n):
+    return lax.div(a, jnp.int32(n))
+
+
+def rem(a, n):
+    return lax.rem(a, jnp.int32(n))
+
+
 def relay_of(head, b, i):
-    p = 2 * b + i // N_Y
-    return ((head + p) % N_Z) * N_Y + (b + i) % N_Y, p
+    p = 2 * b + div(i, N_Y)
+    return rem(head + p, N_Z) * N_Y + rem(b + i, N_Y), p
 
 
 def tile_of(z, y, u):
@@ -102,11 +110,9 @@
     u = lax.axis_index("ulys")
     z = me // N_Y
     y = me % N_Y
-    g_in, b_in, i_in = tile_of(z, y, u)
-    p_out = 2 * b_in + i_in // N_Y
+    g_in, _, i_in = tile_of(z, y, u)
     r_out = i_in % N_Y
     hit1 = jnp.where(g_in == u, 1, 0)
-    hit2 = jnp.where(p_out == u, 1, 0)
 
     small = [
         pltpu.make_async_copy(src, dst, small_sem.at[k])
@@ -120,7 +126,7 @@
     w_copies = [
         pltpu.make_async_copy(w_hbm.at[:, pl.ds(c * WCHUNK, WCHUNK)], w.at[c], w_sem.at[c]) for c in range(N_W)
     ]
-    for copy in x_copies[:1] + small + x_copies[1:] + w_copies:
+    for copy in x_copies:
         copy.start()
 
     barrier = pltpu.get_barrier_semaphore()
@@ -128,15 +134,20 @@
     def greet(grp, ulys):
         pl.semaphore_signal(barrier, inc=1, device_id=(grp, ulys), device_id_type=MESH)
 
-    @pl.loop(0, N_GRP, unroll=8)
-    def _(n):
-        @pl.when(jnp.logical_not((n == me) & (g_in == u)))
-        def _():
-            greet(n, g_in)
-
-    @pl.loop(1, N_ULYS)
+    @pl.loop(1, N_GRP, unroll=True)
     def _(k):
-        greet(me, (u + k) % N_ULYS)
+        greet(rem(me + k, N_GRP), g_in)
+
+    @pl.loop(1, N_ULYS, unroll=True)
+    def _(k):
+        greet(me, rem(u + k, N_ULYS))
+
+    @pl.when(g_in != u)
+    def _():
+        greet(me, g_in)
+
+    for copy in small + w_copies:
+        copy.start()
 
     length = length_s[0]
     done = done_s[0]
@@ -152,8 +163,8 @@
 
         @pl.loop(0, N_GRP)
         def _(k, c=c):
-            b = (k // B_TILES + z + y) % N_B
-            i = (k + y + z) % B_TILES
+            b = rem(div(k, B_TILES) + z + y, N_B)
+            i = rem(k + y + z, B_TILES)
             grp, ulys = relay_of(u, b, i)
             src = heads[c].at[pl.ds(pl.multiple_of(b * QBLK + i * TILE, TILE), TILE)]
             own = (grp == me) & (ulys == u)
@@ -185,22 +196,17 @@
         cols = pl.ds(pl.multiple_of(g_in * FEAT + FIRST[c] * HD, HD), width)
         pltpu.make_async_copy(recv[c], recv[c], recv1.at[c]).wait()
 
-        @pl.loop(0, N_GRP)
+        @pl.loop(0, N_GRP - 1)
         def _(k, c=c, cols=cols):
-            t = k
+            t = rem(k, N_Z) * N_Y + div(k, N_Z) if c + 1 < N_C else k
+            t = jnp.where(t == me, N_GRP - 1, t)
             stage[c][t] = recv[c][source[0, t]]
-            own = (t == me) & (p_out == u)
-
-            @pl.when(own)
-            def _():
-                pltpu.make_async_copy(stage[c].at[t], raw.at[rows, cols], recv2.at[c]).start()
-
-            @pl.when(jnp.logical_not(own))
-            def _():
-                pltpu.make_async_remote_copy(
-                    stage[c].at[t], raw.at[rows, cols], send2.at[c], recv2.at[c],
-                    device_id=(t, p_out), device_id_type=MESH
-                ).start()
+            pltpu.make_async_remote_copy(
+                stage[c].at[t], raw.at[rows, cols], send2.at[c], recv2.at[c], device_id=(t, u), device_id_type=MESH
+            ).start()
+
+        stage[c][me] = recv[c][source[0, me]]
+        pltpu.make_async_copy(stage[c].at[me], raw.at[rows, cols], recv2.at[c]).start()
 
         if c > 0:
             continue
@@ -215,7 +221,7 @@
 
         @pl.loop(1, N_ULYS)
         def _(k):
-            p = (u + k) % N_ULYS
+            p = rem(u + k, N_ULYS)
             pltpu.make_async_remote_copy(
                 part.at[:, pl.ds(pl.multiple_of(p * FEAT, HD), FEAT)],
                 dec_in.at[u], send3, recv3, device_id=(me, p), device_id_type=MESH
@@ -231,16 +237,18 @@
 
     for c in range(N_C):
         pltpu.make_async_copy(recv[c], recv[c], recv2.at[c]).wait()
-    for sems, hit in ((send1, hit1), (send2, hit2)):
-        for c in range(N_C):
-            @pl.when(hit > 0)
-            def _(c=c, sems=sems):
-                sent = stage[c].at[pl.ds(0, N_GRP - 1)]
-                pltpu.make_async_copy(sent, sent, sems.at[c]).wait()
-
-            @pl.when(hit <= 0)
-            def _(c=c, sems=sems):
-                pltpu.make_async_copy(stage[c], stage[c], sems.at[c]).wait()
+    for c in range(N_C):
+        sent = stage[c].at[pl.ds(0, N_GRP - 1)]
+        pltpu.make_async_copy(sent, sent, send2.at[c]).wait()
+
+        @pl.when(hit1 > 0)
+        def _(c=c, sent=sent):
+            pltpu.make_async_copy(sent, sent, send1.at[c]).wait()
+
+        @pl.when(hit1 <= 0)
+        def _(c=c):
+            pltpu.make_async_copy(stage[c], stage[c], send1.at[c]).wait()
+
     sent = dec_in.at[pl.ds(0, N_ULYS - 1)]
     pltpu.make_async_copy(sent, sent, send3).wait()
 
@@ -303,7 +311,7 @@
         + [pltpu.SemaphoreType.DMA((N_C,))] * 4
         + [pltpu.SemaphoreType.DMA] * 2,
         compiler_params=pltpu.CompilerParams(
-            vmem_limit_bytes=VLIM * MIB, collective_id=0, has_side_effects=True
+            vmem_limit_bytes=32 * MIB, collective_id=0, has_side_effects=True
         ),
         name="step",
     )(

time: 44.3 us -> 44.1 us (level); the launches traced: 43.7 us -> 44 us
  no operation moved by 1% of the time
where the time goes in v3:
time: 44.1 us; the launch traced here: 44 us
  Pallas kernels  42 us (95%)
  between operations  1.96 us (4%)
    pallas_call x1, Pallas kernels, body(): pl.pallas_call(step_kernel, out_shape=(pltpu.VMEM((STEPS, FEAT), jnp.bflo...  41 us
    pallas_call x1, Pallas kernels, body(): pl.pallas_call(norm_kernel, out_shape=(jax.ShapeDtypeStruct((STEPS, FEAT)...  1.08 us

profile of v3, /device:TPU:65, one launch (start us, length us, event | category | flops | bytes accessed | tf_op | source)
XLA Modules:
  0.0 44.0 jit_solution(5071759375660907484)
XLA Ops:
  0.6 0.0 copy-start
  1.9 41.0 %step.1 = (bf16[3,640]{1,0:T(4,128)(2,1)S(1)}, bf16[64,5120]{1,0:T(8,128)(2,1)S(1)}) custom-call(bf16[1,512,896]{2,1,0:T(8,128)(2,1)} %x_hbm.1, bf16[3,896]{1,0:T(4,128)(2,1)} %bitcast.5, bf16[640,5120]{1,0:T(8,128)(2,1)} %w_hbm.1, s32[1]{0:T(128)S(6)} %copy.9.length_s, s32[1]{0:T(128)S(6)} %copy.10.done_s, s32[32]{0:T(128)} %assign_hbm.1), custom_call_target="tpu_custom_call" | custom-call | tf_op jit(solution)/shard_map/step/pallas_call | solution.py:286
  42.9 0.0 copy-done
  42.9 1.1 %norm.1 = (bf16[3,640]{1,0:T(4,128)(2,1)}, bf16[64,5120]{1,0:T(8,128)(2,1)}) custom-call(bf16[64,5120]{1,0:T(8,128)(2,1)S(1)} %get-tuple-element.6.raw, bf16[3,640]{1,0:T(4,128)(2,1)S(1)} %get-tuple-element.7.dec, bf16[40,128]{1,0:T(8,128)(2,1)S(1)} %bitcast.4), custom_call_target="tpu_custom_call" | custom-call | tf_op jit(solution)/shard_map/norm/pallas_call | solution.py:321
Async XLA Ops:
  0.6 42.3 %copy-start = (bf16[5120]{0:T(1024)(128)(2,1)S(1)}, bf16[5120]{0:T(1024)(128)(2,1)}, u32[]{:S(2)}) copy-start(bf16[5120]{0:T(1024)(128)(2,1)} %param.10) | copy-start | bytes 30724

commit v4 on v3

--- a/solution.py
+++ b/solution.py
@@ -35,6 +35,8 @@
 
 FIRST = tuple(sum(CHUNKS[:c]) for c in range(len(CHUNKS)))
 N_C = len(CHUNKS)
+ORDER = (0, 1, 4, 2, 5, 8, 3, 6, 9, 7, 10, 11, 12, 13, 14, 15, 28, 29, 30, 31, 24, 25, 26, 27, 16, 17, 18, 19, 20, 21, 22)
+ORDER_LAST = 23
 
 
 def div(a, n):
@@ -102,7 +104,8 @@
         dhead[:, q * HD:(q + 1) * HD] = (o * (1.0 / total)).astype(jnp.bfloat16)
 
 
-def step_kernel(x_hbm, new_hbm, w_hbm, length_s, done_s, assign_hbm, dec, raw, *scratch):
+def step_kernel(x_hbm, new_hbm, w_hbm, length_s, done_s, assign_hbm, dec, *buffers):
+    raw, scratch = buffers[:N_C], buffers[N_C:]
     heads, recv, stage = scratch[:N_C], scratch[N_C:2 * N_C], scratch[2 * N_C:3 * N_C]
     (x, new, w, assign, found, source, fresh, dhead, part, dec_in,
      x_sem, w_sem, small_sem, send1, recv1, send2, recv2, send3, recv3) = scratch[3 * N_C:]
@@ -190,23 +193,27 @@
     to_scalars.start()
     to_scalars.wait()
 
-    rows = pl.ds(pl.multiple_of(r_out * TILE, TILE), TILE)
+    slot = g_in * N_Y + r_out
     for c in range(N_C):
-        width = CHUNKS[c] * HD
-        cols = pl.ds(pl.multiple_of(g_in * FEAT + FIRST[c] * HD, HD), width)
         pltpu.make_async_copy(recv[c], recv[c], recv1.at[c]).wait()
 
-        @pl.loop(0, N_GRP - 1)
-        def _(k, c=c, cols=cols):
-            t = rem(k, N_Z) * N_Y + div(k, N_Z) if c + 1 < N_C else k
-            t = jnp.where(t == me, N_GRP - 1, t)
+        def forward(t, c=c):
             stage[c][t] = recv[c][source[0, t]]
             pltpu.make_async_remote_copy(
-                stage[c].at[t], raw.at[rows, cols], send2.at[c], recv2.at[c], device_id=(t, u), device_id_type=MESH
+                stage[c].at[t], raw[c].at[slot], send2.at[c], recv2.at[c], device_id=(t, u), device_id_type=MESH
             ).start()
 
+        if c + 1 < N_C:
+            @pl.loop(0, N_GRP - 1)
+            def _(k):
+                t = rem(k, N_Z) * N_Y + div(k, N_Z)
+                forward(jnp.where(t == me, N_GRP - 1, t))
+        else:
+            for t in ORDER:
+                forward(jnp.where(me == t, ORDER_LAST, t))
+
         stage[c][me] = recv[c][source[0, me]]
-        pltpu.make_async_copy(stage[c].at[me], raw.at[rows, cols], recv2.at[c]).start()
+        pltpu.make_async_copy(stage[c].at[me], raw[c].at[slot], recv2.at[c]).start()
 
         if c > 0:
             continue
@@ -253,20 +260,23 @@
     pltpu.make_async_copy(sent, sent, send3).wait()
 
 
-def norm_kernel(raw, dec, gain, decoded, scored, out, sem):
+def norm_kernel(*refs):
+    raw = refs[:N_C]
+    dec, gain, decoded, scored, out, sem = refs[N_C:]
     copies = [pltpu.make_async_copy(dec, decoded, sem.at[N_Y])]
     copies[0].start()
     gains = gain[...].astype(jnp.float32)
+    places = [(g, c, j) for g in range(N_ULYS) for c in range(N_C) for j in range(CHUNKS[c])]
     for r in range(N_Y):
         rows = slice(r * TILE, (r + 1) * TILE)
         square = jnp.zeros((TILE, HD), jnp.float32)
-        for k in range(D // HD):
-            lifted = raw[rows, k * HD:(k + 1) * HD].astype(jnp.float32)
+        for g, c, j in places:
+            lifted = raw[c][g * N_Y + r, :, j * HD:(j + 1) * HD].astype(jnp.float32)
             square = square + lifted * lifted
         power = jnp.sum(square, axis=1, keepdims=True) * (1.0 / D)
         factor = lax.rsqrt(power + 1e-06)
-        for k in range(D // HD):
-            lifted = raw[rows, k * HD:(k + 1) * HD].astype(jnp.float32)
+        for k, (g, c, j) in enumerate(places):
+            lifted = raw[c][g * N_Y + r, :, j * HD:(j + 1) * HD].astype(jnp.float32)
             out[rows, k * HD:(k + 1) * HD] = (lifted * factor * gains[k:k + 1]).astype(jnp.bfloat16)
         at = pl.ds(r * TILE, TILE)
         copies.append(pltpu.make_async_copy(out.at[at], scored.at[at], sem.at[r]))
@@ -283,14 +293,13 @@
     def pinned(a):
         return pltpu.with_memory_space_constraint(a, pltpu.HBM)
 
-    dec, raw = pl.pallas_call(
+    dec, *raw = pl.pallas_call(
         step_kernel,
         out_shape=(
             pltpu.VMEM((STEPS, FEAT), jnp.bfloat16),
-            pltpu.VMEM((PBLK, D), jnp.bfloat16),
-        ),
+        ) + tuple(pltpu.VMEM((N_GRP, TILE, n * HD), jnp.bfloat16) for n in CHUNKS),
         in_specs=[hbm] * 3 + [smem] * 2 + [hbm],
-        out_specs=(vmem, vmem),
+        out_specs=(vmem,) * (1 + N_C),
         scratch_shapes=[pltpu.VMEM((CACHE, n * HD), jnp.bfloat16) for n in CHUNKS]
         + [pltpu.VMEM((N_GRP, TILE, n * HD), jnp.bfloat16) for n in CHUNKS] * 2
         + [
@@ -324,12 +333,12 @@
             jax.ShapeDtypeStruct((STEPS, FEAT), jnp.bfloat16),
             jax.ShapeDtypeStruct((PBLK, D), jnp.bfloat16),
         ),
-        in_specs=[vmem] * 3,
+        in_specs=[vmem] * (2 + N_C),
         out_specs=(hbm, hbm),
         scratch_shapes=[pltpu.VMEM((PBLK, D), jnp.bfloat16), pltpu.SemaphoreType.DMA((N_Y + 1,))],
         compiler_params=pltpu.CompilerParams(vmem_limit_bytes=8 * MIB),
         name="norm",
-    )(raw, dec, gain.reshape(D // HD, HD))
+    )(*raw, dec, gain.reshape(D // HD, HD))
     return (decoded.reshape(STEPS, 1, FEAT), scored.reshape(1, PBLK, D))
 
 

time: 44.1 us -> 43.9 us (level); the launches traced: 44 us -> 43.2 us
  Pallas kernels: 42 us -> 41.2 us
    pallas_call x1, Pallas kernels: 41 us -> 40.1 us  [body(): pl.pallas_call(step_kernel, out_shape=(pltpu.VMEM((STEPS, FEAT), jnp.bflo...]
where the time goes in v4:
time: 43.9 us; the launch traced here: 43.2 us
  Pallas kernels  41.2 us (94%)
  between operations  1.96 us (4%)
    pallas_call x1, Pallas kernels, body(): pl.pallas_call(step_kernel, out_shape=(pltpu.VMEM((STEPS, FEAT), jnp.bflo...  40.1 us
    pallas_call x1, Pallas kernels, body(): pl.pallas_call(norm_kernel, out_shape=(jax.ShapeDtypeStruct((STEPS, FEAT)...  1.08 us

profile of v4, /device:TPU:65, one launch (start us, length us, event | category | flops | bytes accessed | tf_op | source)
XLA Modules:
  0.0 43.2 jit_solution(12923453531903114311)
XLA Ops:
  0.6 0.0 copy-start
  1.9 40.1 %step.1 = (bf16[3,640]{1,0:T(4,128)(2,1)S(1)}, bf16[32,16,256]{2,1,0:T(8,128)(2,1)S(1)}, bf16[32,16,384]{2,1,0:T(8,128)(2,1)S(1)}) custom-call(bf16[1,512,896]{2,1,0:T(8,128)(2,1)} %x_hbm.1, bf16[3,896]{1,0:T(4,128)(2,1)} %bitcast.5, bf16[640,5120]{1,0:T(8,128)(2,1)} %w_hbm.1, s32[1]{0:T(128)S(6)} %copy.9.length_s, s32[1]{0:T(128)S(6)} %copy.10.done_s, ...), custom_call_target="tpu_custom_call" | custom-call | tf_op jit(solution)/shard_map/step/pallas_call | solution.py:296
  42.1 0.0 copy-done
  42.1 1.1 %norm.1 = (bf16[3,640]{1,0:T(4,128)(2,1)}, bf16[64,5120]{1,0:T(8,128)(2,1)}) custom-call(bf16[32,16,256]{2,1,0:T(8,128)(2,1)S(1)} %get-tuple-element.7.refs_0_, bf16[32,16,384]{2,1,0:T(8,128)(2,1)S(1)} %get-tuple-element.8.refs_1_, bf16[3,640]{1,0:T(4,128)(2,1)S(1)} %get-tuple-element.9.refs_2_, bf16[40,128]{1,0:T(8,128)(2,1)S(1)} %bitcast.4), custom_call_target="tpu_custom_call" | custom-call | tf_op jit(solution)/shard_map/norm/pallas_call | solution.py:330
Async XLA Ops:
  0.6 41.5 %copy-start = (bf16[5120]{0:T(1024)(128)(2,1)S(1)}, bf16[5120]{0:T(1024)(128)(2,1)}, u32[]{:S(2)}) copy-start(bf16[5120]{0:T(1024)(128)(2,1)} %param.10) | copy-start | bytes 30724

commit v5 on v4

--- a/solution.py
+++ b/solution.py
@@ -35,7 +35,7 @@
 
 FIRST = tuple(sum(CHUNKS[:c]) for c in range(len(CHUNKS)))
 N_C = len(CHUNKS)
-ORDER = (0, 1, 4, 2, 5, 8, 3, 6, 9, 7, 10, 11, 12, 13, 14, 15, 28, 29, 30, 31, 24, 25, 26, 27, 16, 17, 18, 19, 20, 21, 22)
+ORDER = (0, 3, 4, 1, 7, 8, 2, 11, 5, 6, 9, 10, 12, 13, 14, 15, 28, 29, 30, 31, 24, 25, 26, 27, 16, 17, 18, 19, 20, 21, 22)
 ORDER_LAST = 23
 
 
@@ -104,7 +104,7 @@
         dhead[:, q * HD:(q + 1) * HD] = (o * (1.0 / total)).astype(jnp.bfloat16)
 
 
-def step_kernel(x_hbm, new_hbm, w_hbm, length_s, done_s, assign_hbm, dec, *buffers):
+def step_kernel(x_hbm, new_hbm, w_hbm, length_s, done_s, assign_hbm, dec, squares, *buffers):
     raw, scratch = buffers[:N_C], buffers[N_C:]
     heads, recv, stage = scratch[:N_C], scratch[N_C:2 * N_C], scratch[2 * N_C:3 * N_C]
     (x, new, w, assign, found, source, fresh, dhead, part, dec_in,
@@ -244,6 +244,15 @@
 
     for c in range(N_C):
         pltpu.make_async_copy(recv[c], recv[c], recv2.at[c]).wait()
+        if c > 0:
+            continue
+        for r in range(N_Y):
+            square = jnp.zeros((TILE, HD), jnp.float32)
+            for g in range(N_ULYS):
+                for j in range(CHUNKS[c]):
+                    lifted = raw[c][g * N_Y + r, :, j * HD:(j + 1) * HD].astype(jnp.float32)
+                    square = square + lifted * lifted
+            squares[r * TILE:(r + 1) * TILE, :] = square
     for c in range(N_C):
         sent = stage[c].at[pl.ds(0, N_GRP - 1)]
         pltpu.make_async_copy(sent, sent, send2.at[c]).wait()
@@ -262,15 +271,17 @@
 
 def norm_kernel(*refs):
     raw = refs[:N_C]
-    dec, gain, decoded, scored, out, sem = refs[N_C:]
+    dec, squares, gain, decoded, scored, out, sem = refs[N_C:]
     copies = [pltpu.make_async_copy(dec, decoded, sem.at[N_Y])]
     copies[0].start()
     gains = gain[...].astype(jnp.float32)
     places = [(g, c, j) for g in range(N_ULYS) for c in range(N_C) for j in range(CHUNKS[c])]
     for r in range(N_Y):
         rows = slice(r * TILE, (r + 1) * TILE)
-        square = jnp.zeros((TILE, HD), jnp.float32)
+        square = squares[rows, :]
         for g, c, j in places:
+            if c == 0:
+                continue
             lifted = raw[c][g * N_Y + r, :, j * HD:(j + 1) * HD].astype(jnp.float32)
             square = square + lifted * lifted
         power = jnp.sum(square, axis=1, keepdims=True) * (1.0 / D)
@@ -293,13 +304,14 @@
     def pinned(a):
         return pltpu.with_memory_space_constraint(a, pltpu.HBM)
 
-    dec, *raw = pl.pallas_call(
+    dec, squares, *raw = pl.pallas_call(
         step_kernel,
         out_shape=(
             pltpu.VMEM((STEPS, FEAT), jnp.bfloat16),
+            pltpu.VMEM((PBLK, HD), jnp.float32),
         ) + tuple(pltpu.VMEM((N_GRP, TILE, n * HD), jnp.bfloat16) for n in CHUNKS),
         in_specs=[hbm] * 3 + [smem] * 2 + [hbm],
-        out_specs=(vmem,) * (1 + N_C),
+        out_specs=(vmem,) * (2 + N_C),
         scratch_shapes=[pltpu.VMEM((CACHE, n * HD), jnp.bfloat16) for n in CHUNKS]
         + [pltpu.VMEM((N_GRP, TILE, n * HD), jnp.bfloat16) for n in CHUNKS] * 2
         + [
@@ -333,12 +345,12 @@
             jax.ShapeDtypeStruct((STEPS, FEAT), jnp.bfloat16),
             jax.ShapeDtypeStruct((PBLK, D), jnp.bfloat16),
         ),
-        in_specs=[vmem] * (2 + N_C),
+        in_specs=[vmem] * (3 + N_C),
         out_specs=(hbm, hbm),
         scratch_shapes=[pltpu.VMEM((PBLK, D), jnp.bfloat16), pltpu.SemaphoreType.DMA((N_Y + 1,))],
         compiler_params=pltpu.CompilerParams(vmem_limit_bytes=8 * MIB),
         name="norm",
-    )(*raw, dec, gain.reshape(D // HD, HD))
+    )(*raw, dec, squares, gain.reshape(D // HD, HD))
     return (decoded.reshape(STEPS, 1, FEAT), scored.reshape(1, PBLK, D))
 
 

time: 43.9 us -> 43.9 us (level)
  no operation moved by 1% of the time
where the time goes in v5:
time: 43.9 us; the launch traced here: 43.1 us
  Pallas kernels  41.1 us (94%)
  between operations  1.96 us (4%)
    pallas_call x1, Pallas kernels, body(): pl.pallas_call(step_kernel, out_shape=(pltpu.VMEM((STEPS, FEAT), jnp.bflo...  40.1 us
    pallas_call x1, Pallas kernels, body(): pl.pallas_call(norm_kernel, out_shape=(jax.ShapeDtypeStruct((STEPS, FEAT)...  1.04 us

profile of v5, /device:TPU:65, one launch (start us, length us, event | category | flops | bytes accessed | tf_op | source)
XLA Modules:
  0.0 43.1 jit_solution(3481224812964558974)
XLA Ops:
  0.6 0.0 copy-start
  1.9 40.1 %step.1 = (bf16[3,640]{1,0:T(4,128)(2,1)S(1)}, f32[64,128]{1,0:T(8,128)S(1)}, bf16[32,16,256]{2,1,0:T(8,128)(2,1)S(1)}, bf16[32,16,384]{2,1,0:T(8,128)(2,1)S(1)}) custom-call(bf16[1,512,896]{2,1,0:T(8,128)(2,1)} %x_hbm.1, bf16[3,896]{1,0:T(4,128)(2,1)} %bitcast.5, bf16[640,5120]{1,0:T(8,128)(2,1)} %w_hbm.1, s32[1]{0:T(128)S(6)} %copy.9.length_s, ...), custom_call_target="tpu_custom_call" | custom-call | tf_op jit(solution)/shard_map/step/pallas_call | solution.py:307
  42.1 0.0 copy-done
  42.1 1.0 %norm.1 = (bf16[3,640]{1,0:T(4,128)(2,1)}, bf16[64,5120]{1,0:T(8,128)(2,1)}) custom-call(bf16[32,16,256]{2,1,0:T(8,128)(2,1)S(1)} %get-tuple-element.8.refs_0_, bf16[32,16,384]{2,1,0:T(8,128)(2,1)S(1)} %get-tuple-element.9.refs_1_, bf16[3,640]{1,0:T(4,128)(2,1)S(1)} %get-tuple-element.10.refs_2_, f32[64,128]{1,0:T(8,128)S(1)} %get-tuple-element.11.refs_3_, ...), custom_call_target="tpu_custom_call" | custom-call | tf_op jit(solution)/shard_map/norm/pallas_call | solution.py:342
Async XLA Ops:
  0.6 41.4 %copy-start = (bf16[5120]{0:T(1024)(128)(2,1)S(1)}, bf16[5120]{0:T(1024)(128)(2,1)}, u32[]{:S(2)}) copy-start(bf16[5120]{0:T(1024)(128)(2,1)} %param.10) | copy-start | bytes 30724

commit v6 on v4

--- a/solution.py
+++ b/solution.py
@@ -149,7 +149,7 @@
     def _():
         greet(me, g_in)
 
-    for copy in small + w_copies:
+    for copy in small:
         copy.start()
 
     length = length_s[0]
@@ -182,6 +182,8 @@
                     src, recv[c].at[me], send1.at[c], recv1.at[c], device_id=(grp, ulys), device_id_type=MESH
                 ).start()
 
+    for copy in w_copies:
+        copy.start()
     small[0].wait()
     place = lax.broadcasted_iota(jnp.int32, (N_GRP, HD), 0)
     group = jnp.zeros((N_GRP, HD), jnp.int32)

time: 43.9 us -> 43.9 us (level)
  no operation moved by 1% of the time
where the time goes in v6:
time: 43.9 us; the launch traced here: 43.2 us
  Pallas kernels  41.2 us (94%)
  between operations  1.96 us (4%)
    pallas_call x1, Pallas kernels, body(): pl.pallas_call(step_kernel, out_shape=(pltpu.VMEM((STEPS, FEAT), jnp.bflo...  40.1 us
    pallas_call x1, Pallas kernels, body(): pl.pallas_call(norm_kernel, out_shape=(jax.ShapeDtypeStruct((STEPS, FEAT)...  1.08 us

profile of v6, /device:TPU:65, one launch (start us, length us, event | category | flops | bytes accessed | tf_op | source)
XLA Modules:
  0.0 43.2 jit_solution(17098131518488118984)
XLA Ops:
  0.6 0.0 copy-start
  1.9 40.1 %step.1 = (bf16[3,640]{1,0:T(4,128)(2,1)S(1)}, bf16[32,16,256]{2,1,0:T(8,128)(2,1)S(1)}, bf16[32,16,384]{2,1,0:T(8,128)(2,1)S(1)}) custom-call(bf16[1,512,896]{2,1,0:T(8,128)(2,1)} %x_hbm.1, bf16[3,896]{1,0:T(4,128)(2,1)} %bitcast.5, bf16[640,5120]{1,0:T(8,128)(2,1)} %w_hbm.1, s32[1]{0:T(128)S(6)} %copy.9.length_s, s32[1]{0:T(128)S(6)} %copy.10.done_s, ...), custom_call_target="tpu_custom_call" | custom-call | tf_op jit(solution)/shard_map/step/pallas_call | solution.py:298
  42.1 0.0 copy-done
  42.1 1.1 %norm.1 = (bf16[3,640]{1,0:T(4,128)(2,1)}, bf16[64,5120]{1,0:T(8,128)(2,1)}) custom-call(bf16[32,16,256]{2,1,0:T(8,128)(2,1)S(1)} %get-tuple-element.7.refs_0_, bf16[32,16,384]{2,1,0:T(8,128)(2,1)S(1)} %get-tuple-element.8.refs_1_, bf16[3,640]{1,0:T(4,128)(2,1)S(1)} %get-tuple-element.9.refs_2_, bf16[40,128]{1,0:T(8,128)(2,1)S(1)} %bitcast.4), custom_call_target="tpu_custom_call" | custom-call | tf_op jit(solution)/shard_map/norm/pallas_call | solution.py:332
Async XLA Ops:
  0.6 41.5 %copy-start = (bf16[5120]{0:T(1024)(128)(2,1)S(1)}, bf16[5120]{0:T(1024)(128)(2,1)}, u32[]{:S(2)}) copy-start(bf16[5120]{0:T(1024)(128)(2,1)} %param.10) | copy-start | bytes 30724

commit v7 on v6

--- a/solution.py
+++ b/solution.py
@@ -35,7 +35,7 @@
 
 FIRST = tuple(sum(CHUNKS[:c]) for c in range(len(CHUNKS)))
 N_C = len(CHUNKS)
-ORDER = (0, 1, 4, 2, 5, 8, 3, 6, 9, 7, 10, 11, 12, 13, 14, 15, 28, 29, 30, 31, 24, 25, 26, 27, 16, 17, 18, 19, 20, 21, 22)
+ORDER = (0, 3, 4, 1, 7, 8, 2, 11, 5, 6, 9, 10, 12, 13, 14, 15, 28, 29, 30, 31, 24, 25, 26, 27, 16, 17, 18, 19, 20, 21, 22)
 ORDER_LAST = 23
 
 

time: 43.9 us -> 44 us (level)
  no operation moved by 1% of the time
where the time goes in v7:
time: 44 us; the launch traced here: 43.2 us
  Pallas kernels  41.2 us (94%)
  between operations  1.96 us (4%)
    pallas_call x1, Pallas kernels, body(): pl.pallas_call(step_kernel, out_shape=(pltpu.VMEM((STEPS, FEAT), jnp.bflo...  40.1 us
    pallas_call x1, Pallas kernels, body(): pl.pallas_call(norm_kernel, out_shape=(jax.ShapeDtypeStruct((STEPS, FEAT)...  1.08 us

profile of v7, /device:TPU:65, one launch (start us, length us, event | category | flops | bytes accessed | tf_op | source)
XLA Modules:
  0.0 43.2 jit_solution(2292250291032187689)
XLA Ops:
  0.6 0.0 copy-start
  1.9 40.1 %step.1 = (bf16[3,640]{1,0:T(4,128)(2,1)S(1)}, bf16[32,16,256]{2,1,0:T(8,128)(2,1)S(1)}, bf16[32,16,384]{2,1,0:T(8,128)(2,1)S(1)}) custom-call(bf16[1,512,896]{2,1,0:T(8,128)(2,1)} %x_hbm.1, bf16[3,896]{1,0:T(4,128)(2,1)} %bitcast.5, bf16[640,5120]{1,0:T(8,128)(2,1)} %w_hbm.1, s32[1]{0:T(128)S(6)} %copy.9.length_s, s32[1]{0:T(128)S(6)} %copy.10.done_s, ...), custom_call_target="tpu_custom_call" | custom-call | tf_op jit(solution)/shard_map/step/pallas_call | solution.py:298
  42.1 0.0 copy-done
  42.1 1.1 %norm.1 = (bf16[3,640]{1,0:T(4,128)(2,1)}, bf16[64,5120]{1,0:T(8,128)(2,1)}) custom-call(bf16[32,16,256]{2,1,0:T(8,128)(2,1)S(1)} %get-tuple-element.7.refs_0_, bf16[32,16,384]{2,1,0:T(8,128)(2,1)S(1)} %get-tuple-element.8.refs_1_, bf16[3,640]{1,0:T(4,128)(2,1)S(1)} %get-tuple-element.9.refs_2_, bf16[40,128]{1,0:T(8,128)(2,1)S(1)} %bitcast.4), custom_call_target="tpu_custom_call" | custom-call | tf_op jit(solution)/shard_map/norm/pallas_call | solution.py:332
Async XLA Ops:
  0.6 41.4 %copy-start = (bf16[5120]{0:T(1024)(128)(2,1)S(1)}, bf16[5120]{0:T(1024)(128)(2,1)}, u32[]{:S(2)}) copy-start(bf16[5120]{0:T(1024)(128)(2,1)} %param.10) | copy-start | bytes 30724
